TPU v7x, 32 devices: a whole 2x2x4 slice. The times are simulated.
32 devices in a mesh: chan: 16 (over z, y, x), tm: 2 (over core).
Axes of the slice: x: 2, y: 2, z: 4, core: 2. Of those that a mesh axis runs over, the one named last changes fastest.
Arguments:
- filterbank: bfloat16 [8, 4096, 8192], P(None, 'chan', 'tm'), may hold values from -6 to 6
- delays: int32 [12, 1024], P(None, 'chan'), may hold values from 0 to 2
- widths: int32 [8], replicated, may hold values from 1 to 128, as said below
Outputs:
- dedispersed: float32 [8, 1024, 8192], P(None, 'chan', 'tm')
- box_peaks: float32 [8, 8, 1024, 64], P(None, None, 'chan', 'tm')
Inputs may be any that keep to these rules, and one draw needn't show every extreme that they name: widths[w] lies in [2^w, 2^(w+1)) for w below 7; the last equals 128.
All inputs are finite; a program needn't handle non-finite values.
Results may differ from a plain program's by a relative error of at most 0.0003.
Values sent between devices are 32-bit elements; how exact they have to be, the bound alone decides.
A program may use at most 192 MiB of HBM per device.

v0:
```python
import math

import jax
import jax.numpy as jnp
from jax import lax
from jax.sharding import PartitionSpec as P

CHANS = 4096
TILE = 128
DMAX = 2


def shifted(array, axis, by):
    devices = lax.axis_size(axis)
    pairs = [(i, i + by) for i in range(devices) if 0 <= i + by < devices]
    return lax.ppermute(array, axis, pairs)


def partner_2(value, axis, stride):
    mask = 2**stride
    pairs = [(source, source ^ mask) for source in range(lax.axis_size(axis))]
    return lax.ppermute(value, axis, pairs)


def delayed(upper_half, lag_table, copies, trial_axis):
    length = upper_half.shape[-1]
    rim_cells = shifted(upper_half[..., : DMAX * TILE], "tm", -1)
    extended = jnp.concatenate([upper_half, rim_cells], axis=-1)
    extended = jnp.concatenate([extended] * copies, axis=trial_axis)
    result = jnp.zeros(extended.shape[:-1] + (length,), jnp.float32)
    for offset_tiles in range(DMAX + 1):
        window = extended[..., offset_tiles * TILE : offset_tiles * TILE + length]
        result = jnp.where(lag_table[..., None] == offset_tiles, window, result)
    return result


def box_peaks_of(series, widths):
    beams = series.shape[0]
    trials = series.shape[1]
    length = series.shape[2]
    tiles = length // TILE
    rim_cells = shifted(series[..., :TILE], "tm", -1)
    extended = jnp.concatenate([series, rim_cells], axis=-1)
    current_tile = series.reshape(beams, trials, tiles, TILE)
    next_tile = extended[..., TILE:].reshape(beams, trials, tiles, TILE)
    paired = jnp.concatenate([current_tile, next_tile], axis=-1)
    gap = jnp.arange(2 * TILE)[:, None] - jnp.arange(TILE)[None, :]
    peak_list = []
    for width_number in range(widths.shape[0]):
        span_now = widths[width_number]
        band_matrix = ((gap >= 0) & (gap < span_now)).astype(jnp.float32)
        sums = jnp.einsum("brtu,uv->brtv", paired, band_matrix, precision=lax.Precision.HIGHEST)
        scaled = sums * (1.0 / jnp.sqrt(span_now.astype(jnp.float32)))
        peak_list.append(jnp.max(scaled, axis=-1))
    return jnp.stack(peak_list)


def shards(filterbank, delays, widths):
    beams = filterbank.shape[0]
    local_chans = filterbank.shape[1]
    length = filterbank.shape[2]
    devices = lax.axis_size("chan")
    position = lax.axis_index("chan")
    local_sections = local_chans.bit_length() - 1
    cross_sections = devices.bit_length() - 1
    current = filterbank.astype(jnp.float32)[:, :, None, :]
    for section in range(1, local_sections + 1):
        subbands = current.shape[1]
        trials = current.shape[2]
        new_trials = max(1, 2 ** (section - 2))
        copies = new_trials // trials
        pairs = current.reshape(beams, subbands // 2, 2, trials, length)
        lag_row = delays[section - 1]
        if section == 1:
            lag_table = jnp.repeat(lag_row, 2)[:, None]
        else:
            lag_table = lag_row.reshape(subbands // 2, new_trials)
        lower_half = jnp.concatenate([pairs[:, :, 0]] * copies, axis=2)
        current = lower_half + delayed(pairs[:, :, 1], lag_table[None], copies, 2)
    own_trials = current.shape[2]
    for merge_level in range(cross_sections):
        partner = partner_2(current, "chan", merge_level)
        is_upper = jnp.right_shift(position, merge_level) % 2 == 1
        lower_half = jnp.where(is_upper, partner, current)
        upper_half = jnp.where(is_upper, current, partner)
        lag_row = delays[local_sections + merge_level]
        current = lower_half + delayed(upper_half, lag_row[None, None, :], 1, 2)
    current = current.reshape(beams, own_trials, length)
    dedispersed = current * jnp.float32(1.0 / math.sqrt(CHANS))
    return (dedispersed, box_peaks_of(dedispersed, widths))


def solution(mesh):
    return jax.shard_map(
        shards,
        mesh=mesh,
        in_specs=(P(None, "chan", "tm"), P(None, "chan"), P()),
        out_specs=(P(None, "chan", "tm"), P(None, None, "chan", "tm")),
        check_vma=False,
    )
```

profile of v0, /device:TPU:0, one launch (start us, length us, event | category | flops | bytes accessed | tf_op | source)
XLA Modules:
  0.0 1366.8 jit_solution(3650637664696691023)
XLA Ops:
  0.6 18.5 %copy.80 = bf16[8,256,4096]{2,0,1:T(8,128)(2,1)} copy(bf16[8,256,4096]{2,1,0:T(8,128)(2,1)} %param.3) | data formatting | bytes 33554432 | tf_op args[0]
  19.2 9.4 convert.1
  28.6 6.6 slice_bitcast_fusion
  35.2 9.5 copy-done
  50.6 28.1 %fusion.2 = f32[8,128,1,4096]{3,0,1,2:T(8,128)} fusion(f32[8,128,1,4096]{3,0,1,2:T(8,128)} %slice_bitcast_fusion, f32[8,128,1,256]{3,0,1,2:T(8,128)S(1)} %collective-permute-done, f32[8,128,2,1,4096]{4,0,2,1,3:T(8,128)} %copy-done, pred[128]{0:T(512)(128)(4,1)S(1)} %eq.467, pred[128]{0:T(512)(128)(4,1)S(1)} %eq.463, pred[128]{0:T(512)(128)(4,1)S(1)} %eq.459), kind=kLoop, calls=%fused_computation.4 | loop fusion | flops 25165824 | bytes 51380608 | tf_op jit(solution)/shard_map/add | solution.py:79
  78.7 3.9 slice_bitcast_fusion.2
  82.6 3.4 copy-done.3
  87.3 2.5 collective-permute-done.1
  89.8 15.7 %fusion.19 = f32[8,64,1,4096]{3,0,1,2:T(8,128)} fusion(f32[8,64,1,4096]{3,0,1,2:T(8,128)} %copy-done.3, f32[8,64,1,256]{3,0,1,2:T(8,128)S(1)} %collective-permute-done.1, f32[8,64,2,1,4096]{4,0,2,1,3:T(8,128)} %bitcast.195, pred[64]{0:T(512)(128)(4,1)S(1)} %get-tuple-element.42, pred[64]{0:T(512)(128)(4,1)S(1)} %get-tuple-element.41, ...), kind=kLoop, calls=%fused_computation.40 | loop fusion | flops 12582912 | bytes 25690304 | tf_op jit(solution)/shard_map/add | solution.py:79
  105.5 6.2 slice_bitcast_fusion.13
  111.8 1.9 copy-done.6
  117.1 4.1 maximum_maximum_fusion
  121.2 5.9 fusion.42
  127.1 3.9 copy.87
  131.5 2.0 collective-permute-start.3
  134.4 2.2 copy_bitcast_fusion.1
  137.4 9.4 fusion.39
  146.8 6.2 slice_bitcast_fusion.10
  152.9 2.0 copy-done.7
  158.4 3.9 maximum_maximum_fusion.2
  162.3 9.3 fusion.36
  171.6 8.2 copy.90
  180.3 1.9 copy-done.4
  184.0 2.6 slice.348
  186.6 2.4 copy.117
  189.8 4.9 fusion.33
  194.7 6.2 slice_bitcast_fusion.7
  200.8 2.0 copy-done.8
  204.4 1.9 collective-permute-done.6
  206.3 4.0 maximum_maximum_fusion.4
  210.3 7.0 fusion.30
  217.2 6.2 slice_bitcast_fusion.5
  224.7 2.1 collective-permute-done.7
  227.6 8.2 fusion.26
  235.8 2.9 collective-permute-start.8
  238.8 181.1 %collective-permute-done.8 = f32[8,1,64,4096]{3,2,0,1:T(8,128)} collective-permute-done((f32[8,1,64,4096]{3,2,0,1:T(8,128)}, f32[8,1,64,4096]{3,2,0,1:T(8,128)}, u32[]{:S(2)}, u32[]{:S(2)}) %collective-permute-start.8) | collective-permute-done | bytes 8388640 | tf_op jit(solution)/shard_map/ppermute | solution.py:22
  419.8 8.7 broadcast_select_fusion
  431.2 2.3 collective-permute-done.9
  433.5 15.0 %fusion.16 = f32[8,1,64,4096]{3,2,0,1:T(8,128)} fusion(f32[8,1,64,4096]{3,2,0,1:T(8,128)} %broadcast_select_fusion, f32[8,1,64,256]{3,2,0,1:T(8,128)S(1)} %collective-permute-done.9, f32[8,1,64,4096]{3,2,0,1:T(8,128)} %collective-permute-done.8, f32[8,1,64,4096]{3,2,0,1:T(8,128)} %fusion.26, pred[64]{0:T(512)(128)(4,1)S(1)} %copy-done.22, ...), kind=kLoop, calls=%fused_computation.37 | loop fusion | flops 14680064 | bytes 34078912 | tf_op jit(solution)/shard_map/add | solution.py:87
  450.3 181.1 %collective-permute-done.10 = f32[8,1,64,4096]{3,2,0,1:T(8,128)} collective-permute-done((f32[8,1,64,4096]{3,2,0,1:T(8,128)}, f32[8,1,64,4096]{3,2,0,1:T(8,128)}, u32[]{:S(2)}, u32[]{:S(2)}) %collective-permute-start.10) | collective-permute-done | bytes 8388640 | tf_op jit(solution)/shard_map/ppermute | solution.py:22
  631.3 8.7 broadcast_select_fusion.1
  642.5 2.5 collective-permute-done.11
  645.0 15.0 %fusion.13 = f32[8,1,64,4096]{3,2,0,1:T(8,128)} fusion(f32[8,1,64,4096]{3,2,0,1:T(8,128)} %broadcast_select_fusion.1, f32[8,1,64,256]{3,2,0,1:T(8,128)S(1)} %collective-permute-done.11, f32[8,1,64,4096]{3,2,0,1:T(8,128)} %collective-permute-done.10, f32[8,1,64,4096]{3,2,0,1:T(8,128)} %fusion.16, pred[64]{0:T(512)(128)(4,1)S(1)} %copy-done.19, ...), kind=kLoop, calls=%fused_computation.34 | loop fusion | flops 14680064 | bytes 34078912 | tf_op jit(solution)/shard_map/add | solution.py:87
  661.8 181.1 %collective-permute-done.12 = f32[8,1,64,4096]{3,2,0,1:T(8,128)} collective-permute-done((f32[8,1,64,4096]{3,2,0,1:T(8,128)}, f32[8,1,64,4096]{3,2,0,1:T(8,128)}, u32[]{:S(2)}, u32[]{:S(2)}) %collective-permute-start.12) | collective-permute-done | bytes 8388640 | tf_op jit(solution)/shard_map/ppermute | solution.py:22
  842.9 8.7 broadcast_select_fusion.2
  854.0 2.5 collective-permute-done.13
  856.5 15.0 %fusion.10 = f32[8,1,64,4096]{3,2,0,1:T(8,128)} fusion(f32[8,1,64,4096]{3,2,0,1:T(8,128)} %broadcast_select_fusion.2, f32[8,1,64,256]{3,2,0,1:T(8,128)S(1)} %collective-permute-done.13, f32[8,1,64,4096]{3,2,0,1:T(8,128)} %collective-permute-done.12, f32[8,1,64,4096]{3,2,0,1:T(8,128)} %fusion.13, pred[64]{0:T(512)(128)(4,1)S(1)} %copy-done.17, ...), kind=kLoop, calls=%fused_computation.31 | loop fusion | flops 14680064 | bytes 34078912 | tf_op jit(solution)/shard_map/add | solution.py:87
  871.6 2.8 collective-permute-start.14
  874.3 360.8 %collective-permute-done.14 = f32[8,1,64,4096]{3,2,0,1:T(8,128)} collective-permute-done((f32[8,1,64,4096]{3,2,0,1:T(8,128)}, f32[8,1,64,4096]{3,2,0,1:T(8,128)}, u32[]{:S(2)}, u32[]{:S(2)}) %collective-permute-start.14) | collective-permute-done | bytes 8388640 | tf_op jit(solution)/shard_map/ppermute | solution.py:22
  1235.1 8.7 broadcast_select_fusion.3
  1252.3 11.8 fusion.7
  1265.7 5.1 copy.113
  1270.8 4.5 bitcast_dynamic-update-slice_fusion.1
  1275.3 7.6 pad_maximum_fusion.1
  1283.0 8.4 copy.114
  1291.4 4.5 bitcast_dynamic-update-slice_fusion
  1295.9 9.0 multiply_reduce_fusion.7
  1304.9 8.4 multiply_reduce_fusion.6
  1313.3 8.6 multiply_reduce_fusion.5
  1321.9 8.5 multiply_reduce_fusion.4
  1330.4 8.6 multiply_reduce_fusion.3
  1339.0 8.5 multiply_reduce_fusion.2
  1347.5 8.6 multiply_reduce_fusion.1
  1356.2 8.4 multiply_reduce_fusion
  (117 shorter events, 39.9 us)
Async XLA Ops:
  28.6 16.1 %copy-start = (f32[8,128,2,1,4096]{4,0,2,1,3:T(8,128)}, f32[8,128,2,1,4096]{4,0,2,1,3:T(8,128)S(1)}, u32[]{:S(2)}) copy-start(f32[8,128,2,1,4096]{4,0,2,1,3:T(8,128)S(1)} %convert.1) | copy-start | bytes 100663296
  28.6 18.7 %copy-start.11 = (s32[12,64]{1,0:T(8,128)S(1)}, s32[12,64]{1,0:T(8,128)}, u32[]{:S(2)}) copy-start(s32[12,64]{1,0:T(8,128)} %param.4) | copy-start | bytes 9220
  46.0 4.6 collective-permute-start
  82.6 3.4 copy-start.3
  86.0 3.8 collective-permute-start.1
  111.8 1.9 copy-start.6
  113.7 3.4 collective-permute-start.2
  116.0 5.3 copy-start.9
  131.0 3.4 copy-start.2
  131.5 5.1 collective-permute-start.3
  152.9 2.0 copy-start.7
  155.0 3.4 collective-permute-start.4
  180.3 1.9 copy-start.4
  182.2 6.8 collective-permute-start.5
  184.0 5.1 copy-start.5
  200.8 2.0 copy-start.8
  202.9 3.4 collective-permute-start.6
  223.4 3.4 collective-permute-start.7
  235.8 184.0 %collective-permute-start.8 = (f32[8,1,64,4096]{3,2,0,1:T(8,128)}, f32[8,1,64,4096]{3,2,0,1:T(8,128)}, u32[]{:S(2)}, u32[]{:S(2)}) collective-permute-start(f32[8,1,64,4096]{3,2,0,1:T(8,128)} %fusion.26), channel_id=1, source_target_pairs={{0,2},{2,0},{4,6},{6,4},{8,10},{10,8},{12,14},{14,12},{16,18},{18,... | collective-permute-start | bytes 25165832 | tf_op jit(solution)/shard_map/ppermute | solution.py:22
  238.7 194.7 %copy-start.21 = (pred[64]{0:T(512)(128)(4,1)S(1)}, pred[64]{0:T(512)(128)(4,1)}, u32[]{:S(2)}) copy-start(pred[64]{0:T(512)(128)(4,1)} %get-tuple-element.30) | copy-start | bytes 196
  238.7 194.7 %copy-start.22 = (pred[64]{0:T(512)(128)(4,1)S(1)}, pred[64]{0:T(512)(128)(4,1)}, u32[]{:S(2)}) copy-start(pred[64]{0:T(512)(128)(4,1)} %get-tuple-element.31) | copy-start | bytes 196
  238.7 194.7 %copy-start.23 = (pred[64]{0:T(512)(128)(4,1)S(1)}, pred[64]{0:T(512)(128)(4,1)}, u32[]{:S(2)}) copy-start(pred[64]{0:T(512)(128)(4,1)} %get-tuple-element.39) | copy-start | bytes 196
  429.6 3.8 collective-permute-start.9
  448.5 182.8 %collective-permute-start.10 = (f32[8,1,64,4096]{3,2,0,1:T(8,128)}, f32[8,1,64,4096]{3,2,0,1:T(8,128)}, u32[]{:S(2)}, u32[]{:S(2)}) collective-permute-start(f32[8,1,64,4096]{3,2,0,1:T(8,128)} %fusion.16), channel_id=1, source_target_pairs={{0,4},{2,6},{4,0},{6,2},{8,12},{10,14},{12,8},{14,10},{16,20},{18,... | collective-permute-start | bytes 25165832 | tf_op jit(solution)/shard_map/ppermute | solution.py:22
  450.3 194.7 %copy-start.18 = (pred[64]{0:T(512)(128)(4,1)S(1)}, pred[64]{0:T(512)(128)(4,1)}, u32[]{:S(2)}) copy-start(pred[64]{0:T(512)(128)(4,1)} %get-tuple-element.32) | copy-start | bytes 196
  450.3 194.7 %copy-start.19 = (pred[64]{0:T(512)(128)(4,1)S(1)}, pred[64]{0:T(512)(128)(4,1)}, u32[]{:S(2)}) copy-start(pred[64]{0:T(512)(128)(4,1)} %get-tuple-element.33) | copy-start | bytes 196
  450.3 194.7 %copy-start.20 = (pred[64]{0:T(512)(128)(4,1)S(1)}, pred[64]{0:T(512)(128)(4,1)}, u32[]{:S(2)}) copy-start(pred[64]{0:T(512)(128)(4,1)} %get-tuple-element.38) | copy-start | bytes 196
  641.2 3.8 collective-permute-start.11
  660.0 182.9 %collective-permute-start.12 = (f32[8,1,64,4096]{3,2,0,1:T(8,128)}, f32[8,1,64,4096]{3,2,0,1:T(8,128)}, u32[]{:S(2)}, u32[]{:S(2)}) collective-permute-start(f32[8,1,64,4096]{3,2,0,1:T(8,128)} %fusion.13), channel_id=1, source_target_pairs={{0,8},{2,10},{4,12},{6,14},{8,0},{10,2},{12,4},{14,6},{16,24},{18,... | collective-permute-start | bytes 25165832 | tf_op jit(solution)/shard_map/ppermute | solution.py:22
  661.8 194.7 %copy-start.12 = (pred[64]{0:T(512)(128)(4,1)S(1)}, pred[64]{0:T(512)(128)(4,1)}, u32[]{:S(2)}) copy-start(pred[64]{0:T(512)(128)(4,1)} %get-tuple-element.46) | copy-start | bytes 196
  661.8 194.7 %copy-start.16 = (pred[64]{0:T(512)(128)(4,1)S(1)}, pred[64]{0:T(512)(128)(4,1)}, u32[]{:S(2)}) copy-start(pred[64]{0:T(512)(128)(4,1)} %get-tuple-element.34) | copy-start | bytes 196
  661.8 194.7 %copy-start.17 = (pred[64]{0:T(512)(128)(4,1)S(1)}, pred[64]{0:T(512)(128)(4,1)}, u32[]{:S(2)}) copy-start(pred[64]{0:T(512)(128)(4,1)} %get-tuple-element.35) | copy-start | bytes 196
  852.7 3.8 collective-permute-start.13
  871.6 363.6 %collective-permute-start.14 = (f32[8,1,64,4096]{3,2,0,1:T(8,128)}, f32[8,1,64,4096]{3,2,0,1:T(8,128)}, u32[]{:S(2)}, u32[]{:S(2)}) collective-permute-start(f32[8,1,64,4096]{3,2,0,1:T(8,128)} %fusion.10), channel_id=1, source_target_pairs={{0,16},{2,18},{4,20},{6,22},{8,24},{10,26},{12,28},{14,30},{16,0},... | collective-permute-start | bytes 25165832 | tf_op jit(solution)/shard_map/ppermute | solution.py:22
  874.3 372.0 %copy-start.10 = (s32[8]{0:T(128)S(1)}, s32[8]{0:T(128)}, u32[]{:S(2)}) copy-start(s32[8]{0:T(128)} %param.5) | copy-start | bytes 100
  874.3 378.0 %copy-start.13 = (pred[64]{0:T(512)(128)(4,1)S(1)}, pred[64]{0:T(512)(128)(4,1)}, u32[]{:S(2)}) copy-start(pred[64]{0:T(512)(128)(4,1)} %get-tuple-element.27) | copy-start | bytes 196
  874.3 378.0 %copy-start.14 = (pred[64]{0:T(512)(128)(4,1)S(1)}, pred[64]{0:T(512)(128)(4,1)}, u32[]{:S(2)}) copy-start(pred[64]{0:T(512)(128)(4,1)} %get-tuple-element.36) | copy-start | bytes 196
  874.3 378.0 %copy-start.15 = (pred[64]{0:T(512)(128)(4,1)S(1)}, pred[64]{0:T(512)(128)(4,1)}, u32[]{:S(2)}) copy-start(pred[64]{0:T(512)(128)(4,1)} %get-tuple-element.37) | copy-start | bytes 196
  1245.0 7.3 collective-permute-start.15
  1264.1 6.7 copy-start.1
  1264.2 11.2 collective-permute-start.16
where the time goes:
time: 1380 us; the launch traced here: 1370 us
  waiting for transfers between devices  922 us (67%)
  other arithmetic  213 us (15%)
  local copies, waits for them, and re-layouts  129 us (9%)
  matrix products  68.6 us (5%)
  starting transfers between devices  27.4 us (2%)
    ppermute x4, waiting for transfers between devices, partner_2(): return lax.ppermute(value, axis, pairs)  904 us
    add x7, other arithmetic, shards(): current = lower_half + delayed(pairs[:, :, 1], lag_table[None], copies, 2)  81.4 us
    dot_general x8, matrix products, box_peaks_of(): jnp.einsum('brtu,uv->brtv', paired, band_matrix, precision=lax.Precision....  68.6 us
    unnamed x61, local copies, waits for them, and re-layouts  62.4 us
    add x3, other arithmetic, shards(): current = lower_half + delayed(upper_half, lag_row[None, None, :], 1, 2)  45.1 us
    select_n x4, other arithmetic, shards(): upper_half = jnp.where(is_upper, current, partner)  35 us
  transfers between devices with their start and end apart: 17, of which 13 were waited for; matrix products, arithmetic and copies ran while one was open for 2% of the time, Pallas kernels for 0%

commit v1 on v0

v1 whole, which is shorter than its diff:
```python
import functools
import math

import jax
import jax.numpy as jnp
import numpy as np
from jax import lax
from jax.experimental import pallas as pl
from jax.experimental.pallas import tpu as pltpu
from jax.sharding import PartitionSpec as P

CHANS = 4096
TILE = 128
DMAX = 2
BLOCK = 1024
MESH = pl.DeviceIdType.MESH


def table_factors(local_chans, rows):
    sections = local_chans.bit_length() - 1
    left = np.zeros((rows, sections, rows), np.float32)
    right = np.zeros((sections, rows, local_chans), np.float32)
    r = np.arange(rows)[:, None]
    j = np.arange(rows)
    c = np.arange(local_chans)[None, :]
    for section in range(1, sections + 1):
        trials = max(1, 2 ** (section - 2))
        left[:, section - 1, :] = (j[None, :] % trials) == (r % trials)
        band = c >> max(section, 2)
        upper = (c >> (section - 1)) & 1
        right[section - 1] = ((j[:, None] // trials) == band) & (upper == 1)
    return left.reshape(rows, -1), right.reshape(-1, local_chans)


def kernel(
    sizes, fb_ref, total_ref, lag_ref, width_ref, out_ref, peak_ref,
    held, rims, box_rim, spill, ext, weight, band, fb,
    send_sem, recv_sem, rim_send, rim_recv, spill_send, spill_recv, in_sem, out_sem,
):
    beams, chans, length, rows, per, merges, times = sizes
    split = rows // per
    chunks = beams * split
    tiles = length // TILE
    depth = DMAX * (chans.bit_length() - 1)
    shifts = depth + 1
    lead = depth * TILE
    rim = DMAX * TILE
    widths = width_ref.shape[0]
    me = lax.axis_index("chan")
    now = lax.axis_index("tm")
    has_left = now > 0
    has_right = now < times - 1
    left = lax.rem(now + times - 1, times)
    right = lax.rem(now + 1, times)
    is_upper = [(me // 2**m) % 2 for m in range(merges)]
    partner = [me + (1 - 2 * is_upper[m]) * 2**m for m in range(merges)]

    barrier = pltpu.get_barrier_semaphore()
    for m in range(merges):
        pl.semaphore_signal(barrier, inc=1, device_id={"chan": partner[m]}, device_id_type=MESH)

    @pl.when(has_left)
    def _():
        pl.semaphore_signal(barrier, inc=1, device_id={"tm": left}, device_id_type=MESH)

    @pl.when(has_right)
    def _():
        pl.semaphore_signal(barrier, inc=1, device_id={"tm": right}, device_id_type=MESH)

    def load(beam):
        slot = lax.rem(beam, 2)
        return pltpu.make_async_copy(fb_ref.at[beam], fb.at[slot], in_sem.at[slot])

    load(0).start()

    for q in range(split):
        total = total_ref[q * per : (q + 1) * per, :]
        for s in range(shifts):
            weight[q, s] = (total == float(s)).astype(jnp.bfloat16)
    gap = lax.broadcasted_iota(jnp.int32, (2 * TILE, TILE), 0) - lax.broadcasted_iota(jnp.int32, (2 * TILE, TILE), 1)
    for w in range(widths):
        band[:, w * TILE : (w + 1) * TILE] = ((gap >= 0) & (gap < width_ref[w])).astype(jnp.float32).astype(jnp.bfloat16)

    @pl.when(jnp.logical_not(has_right))
    def _():
        rims[...] = jnp.zeros_like(rims)
        box_rim[...] = jnp.zeros_like(box_rim)

    peers = merges + jnp.minimum(now, 1) + jnp.minimum(times - 1 - now, 1)
    pl.semaphore_wait(barrier, peers)

    def exchange(m, c):
        return pltpu.make_async_remote_copy(
            src_ref=held.at[0, c], dst_ref=held.at[m + 1, c],
            send_sem=send_sem.at[m, c], recv_sem=recv_sem.at[m, c],
            device_id={"chan": partner[m]}, device_id_type=MESH,
        )

    def rim_copy(m, c):
        slot = (1 - is_upper[m]) * (m + 1)
        return pltpu.make_async_remote_copy(
            src_ref=held.at[slot, c, :, pl.ds(0, rim)], dst_ref=rims.at[m, c],
            send_sem=rim_send.at[m, c], recv_sem=rim_recv.at[m, c],
            device_id={"tm": left}, device_id_type=MESH,
        )

    def box_copy(c):
        return pltpu.make_async_remote_copy(
            src_ref=held.at[0, c, :, pl.ds(0, TILE)], dst_ref=box_rim.at[c],
            send_sem=rim_send.at[merges, c], recv_sem=rim_recv.at[merges, c],
            device_id={"tm": left}, device_id_type=MESH,
        )

    def spill_copy(c):
        return pltpu.make_async_remote_copy(
            src_ref=ext.at[lax.rem(c, 2), :, pl.ds(0, lead)], dst_ref=spill.at[c],
            send_sem=spill_send.at[c], recv_sem=spill_recv.at[c],
            device_id={"tm": left}, device_id_type=MESH,
        )

    def place(c):
        return c // split, pl.ds(pl.multiple_of(lax.rem(c, split) * per, per), per)

    def result(c):
        beam, at = place(c)
        return pltpu.make_async_copy(held.at[0, c], out_ref.at[beam, at, :], out_sem.at[c])

    def local(c):
        beam = c // split
        q = lax.rem(c, split)
        slot = lax.rem(beam, 2)
        side = lax.rem(c, 2)

        @pl.when(q == 0)
        def _():
            load(beam).wait()

            @pl.when(beam + 1 < beams)
            def _():
                load(beam + 1).start()

        @pl.when(jnp.logical_and(has_left, c >= 2))
        def _():
            spill_copy(c - 2).wait_send()

        ext[side] = jnp.zeros(ext.shape[1:], jnp.float32)
        mat = weight[q].reshape(shifts * per, chans)
        step = BLOCK // 2

        def columns(k, carry):
            at = pl.multiple_of(k * step, step)
            part = jnp.dot(mat, fb[slot, :, pl.ds(at, step)], preferred_element_type=jnp.float32)
            for s in range(shifts):
                to = pl.ds(pl.multiple_of(at + (depth - s) * TILE, TILE), step)
                ext[side, :, to] = ext[side, :, to] + part[s * per : (s + 1) * per, :]
            return carry

        lax.fori_loop(0, length // step, columns, 0)

        @pl.when(has_left)
        def _():
            spill_copy(c).start()

        held[0, c] = ext[side, :, lead:]

    def join(c):
        @pl.when(has_right)
        def _():
            spill_copy(c).wait_recv()
            held[0, c, :, length - lead :] = held[0, c, :, length - lead :] + spill[c]

        exchange(0, c).start()

    def arrive(m, c):
        exchange(m, c).wait_recv()

        @pl.when(has_left)
        def _():
            rim_copy(m, c).start()

    def merge(m, c):
        exchange(m, c).wait_send()

        @pl.when(has_left)
        def _():
            rim_copy(m, c).wait_send()

        @pl.when(has_right)
        def _():
            rim_copy(m, c).wait_recv()

        low = is_upper[m] * (m + 1)
        high = (1 - is_upper[m]) * (m + 1)
        _, at = place(c)
        lag = jnp.concatenate([lag_ref[m, at, :]] * (BLOCK // TILE), axis=1)
        last = m == merges - 1
        for start in range(0, length, BLOCK):
            if start + BLOCK < length:
                window = held[high, c, :, start : start + BLOCK + rim]
            else:
                window = jnp.concatenate([held[high, c, :, start : start + BLOCK], rims[m, c]], axis=1)
            moved = window[:, :BLOCK]
            for offset in range(1, DMAX + 1):
                moved = jnp.where(lag == offset, window[:, offset * TILE : offset * TILE + BLOCK], moved)
            new = held[low, c, :, start : start + BLOCK] + moved
            if last:
                new = new * jnp.float32(1.0 / math.sqrt(CHANS))
            held[0, c, :, start : start + BLOCK] = new
        if last:
            result(c).start()

            @pl.when(has_left)
            def _():
                box_copy(c).start()
        else:
            exchange(m + 1, c).start()

    def peaks(c):
        @pl.when(has_right)
        def _():
            box_copy(c).wait_recv()

        beam, at = place(c)
        lane = lax.broadcasted_iota(jnp.int32, (per, TILE), 1)
        found = [jnp.zeros((per, TILE), jnp.float32) for _ in range(widths)]
        group = min(8, tiles)
        for first in range(0, tiles, group):
            start = first * TILE
            if first + group < tiles:
                window = held[0, c, :, start : start + (group + 1) * TILE]
            else:
                window = jnp.concatenate([held[0, c, :, start : start + group * TILE], box_rim[c]], axis=1)
            coarse = window.astype(jnp.bfloat16)
            fine = (window - coarse.astype(jnp.float32)).astype(jnp.bfloat16)
            pairs = [
                jnp.concatenate([part[:, i * TILE : (i + 2) * TILE] for i in range(group)], axis=0)
                for part in (coarse, fine)
            ]
            sums = sum(jnp.dot(pair, band[...], preferred_element_type=jnp.float32) for pair in pairs)
            for w in range(widths):
                best = jnp.max(sums[:, w * TILE : (w + 1) * TILE], axis=1, keepdims=True)
                for i in range(group):
                    found[w] = jnp.where(lane == first + i, best[i * per : (i + 1) * per], found[w])
        for w in range(widths):
            span = jnp.full((per, TILE), width_ref[w], jnp.int32).astype(jnp.float32)
            peak_ref[w, beam, at, :] = (found[w] * (1.0 / jnp.sqrt(span)))[:, :tiles]

    lags = [3 + 2 * m for m in range(merges)]
    lags[-1] += 1
    final = lags[-1] + 1

    def step(i, carry):
        def guarded(lag, action):
            c = i - lag

            @pl.when(jnp.logical_and(c >= 0, c < chunks))
            def _():
                action(c)

        for m in reversed(range(merges)):
            guarded(lags[m], functools.partial(arrive, m))
        guarded(1, join)
        guarded(0, local)
        for m in reversed(range(merges)):
            guarded(lags[m], functools.partial(merge, m))
        guarded(final, peaks)
        return carry

    lax.fori_loop(0, chunks + final, step, 0)

    def drain(c, carry):
        result(c).wait()

        @pl.when(has_left)
        def _():
            box_copy(c).wait_send()

            @pl.when(c >= chunks - 2)
            def _():
                spill_copy(c).wait_send()

        return carry

    lax.fori_loop(0, chunks, drain, 0)


def shards(filterbank, delays, widths):
    beams, chans, length = filterbank.shape
    rows = chans // 4
    per = min(rows, 16)
    chunks = beams * (rows // per)
    local_sections = chans.bit_length() - 1
    merges = lax.axis_size("chan").bit_length() - 1
    times = lax.axis_size("tm")
    tiles = length // TILE
    depth = DMAX * local_sections
    left, right = table_factors(chans, rows)
    table = delays[:local_sections].reshape(-1, 1).astype(jnp.bfloat16) * jnp.asarray(right, jnp.bfloat16)
    total = jnp.dot(jnp.asarray(left, jnp.bfloat16), table, preferred_element_type=jnp.float32)
    lag = jnp.broadcast_to(delays[local_sections:, :, None], (merges, rows, TILE))
    sizes = (beams, chans, length, rows, per, merges, times)
    f32 = jnp.float32
    vmem = pl.BlockSpec(memory_space=pltpu.VMEM)
    hbm = pl.BlockSpec(memory_space=pl.ANY)
    dma = pltpu.SemaphoreType.DMA
    return pl.pallas_call(
        functools.partial(kernel, sizes),
        out_shape=(
            jax.ShapeDtypeStruct((beams, rows, length), f32),
            jax.ShapeDtypeStruct((widths.shape[0], beams, rows, tiles), f32),
        ),
        in_specs=[hbm, vmem, vmem, pl.BlockSpec(memory_space=pltpu.SMEM)],
        out_specs=(hbm, vmem),
        scratch_shapes=[
            pltpu.VMEM((merges + 1, chunks, per, length), f32),
            pltpu.VMEM((merges, chunks, per, DMAX * TILE), f32),
            pltpu.VMEM((chunks, per, TILE), f32),
            pltpu.VMEM((chunks, per, depth * TILE), f32),
            pltpu.VMEM((2, per, depth * TILE + length), f32),
            pltpu.VMEM((rows // per, depth + 1, per, chans), jnp.bfloat16),
            pltpu.VMEM((2 * TILE, widths.shape[0] * TILE), jnp.bfloat16),
            pltpu.VMEM((2, chans, length), jnp.bfloat16),
            dma((merges, chunks)),
            dma((merges, chunks)),
            dma((merges + 1, chunks)),
            dma((merges + 1, chunks)),
            dma((chunks,)),
            dma((chunks,)),
            dma((2,)),
            dma((chunks,)),
        ],
        compiler_params=pltpu.CompilerParams(
            collective_id=0, has_side_effects=True, vmem_limit_bytes=60 * 2**20
        ),
        name="dedisperse",
    )(filterbank, total, lag, widths)


def solution(mesh):
    return jax.shard_map(
        shards,
        mesh=mesh,
        in_specs=(P(None, "chan", "tm"), P(None, "chan"), P()),
        out_specs=(P(None, "chan", "tm"), P(None, None, "chan", "tm")),
        check_vma=False,
    )
```

time: 1380 us -> 426 us (0.31)
  waiting for transfers between devices: 922 us -> 0 us
  Pallas kernels: 0 us -> 410 us
  other arithmetic: 213 us -> 0.69 us
  local copies, waits for them, and re-layouts: 129 us -> 12.5 us
  matrix products: 68.6 us -> 1.89 us
  starting transfers between devices: 27.4 us -> 0 us
    ppermute x17 -> x0, waiting for transfers between devices: 922 us -> none  [the longest x4 904 us: partner_2(): return lax.ppermute(value, axis, pairs)]
    pallas_call x0 -> x1, Pallas kernels: none -> 410 us  [shards(): pl.pallas_call(functools.partial(kernel, sizes), out_shape=(jax.ShapeDtyp...]
    add x10 -> x0, other arithmetic: 127 us -> none  [the longest x7 81.4 us: shards(): current = lower_half + delayed(pairs[:, :, 1], lag_table[None], copies, 2)]
    dot_general x8 -> x1, matrix products: 68.6 us -> 1.89 us  [shards(): jnp.dot(jnp.asarray(left, jnp.bfloat16), table, preferred_element_type=jn...]
    unnamed x61 -> x1, local copies, waits for them, and re-layouts: 62.4 us -> 7.77 us
    squeeze x9 -> x0, local copies, waits for them, and re-layouts: 38.3 us -> none  [the longest x5 26.9 us: shards(): lower_half = jnp.concatenate([pairs[:, :, 0]] * copies, axis=2)]
    select_n x4 -> x0, other arithmetic: 35 us -> none  [shards(): upper_half = jnp.where(is_upper, current, partner)]
    ppermute x17 -> x0, starting transfers between devices: 27.4 us -> none  [the longest x13 18.2 us: shifted(): return lax.ppermute(array, axis, pairs)]
  transfers between devices with their start and end apart: 17 -> 0, of which waited for: 13 -> 0; matrix products, arithmetic and copies ran while one was open for 2% -> 0% of each run, Pallas kernels for 0% -> 0%
where the time goes in v1:
time: 426 us
  Pallas kernels  410 us (96%)
  local copies, waits for them, and re-layouts  12.5 us (3%)
    pallas_call x1, Pallas kernels, shards(): pl.pallas_call(functools.partial(kernel, sizes), out_shape=(jax.ShapeDtyp...  410 us

profile of v1, /device:TPU:0, one launch (start us, length us, event | category | flops | bytes accessed | tf_op | source)
XLA Modules:
  0.0 426.1 jit_solution(8687185502643912750)
XLA Ops:
  0.6 0.7 slice.8
  1.3 0.7 slice_convert_fusion
  2.0 0.1 convert_element_type.9
  2.1 1.9 fusion.total_ref
  4.0 0.8 broadcast_in_dim.2.lag_ref
  4.7 410.4 %dedisperse.1 = (f32[8,64,4096]{2,1,0:T(8,128)}, f32[8,8,64,32]{3,2,1,0:T(8,128)}) custom-call(bf16[8,256,4096]{2,1,0:T(8,128)(2,1)} %fb_ref.1, f32[64,256]{1,0:T(8,128)} %fusion.total_ref, s32[4,64,128]{2,1,0:T(8,128)} %broadcast_in_dim.2.lag_ref, s32[8]{0:T(128)} %width_ref.1), custom_call_target="tpu_custom_call" | custom-call | tf_op jit(solution)/shard_map/dedisperse/pallas_call | solution.py:306
  415.1 3.2 copy.7
  418.3 7.8 %copy.9 = f32[8,64,4096]{2,1,0:T(8,128)} copy(f32[8,64,4096]{2,1,0:T(8,128)} %get-tuple-element.6) | data formatting | bytes 16777216

commit v2 on v1

--- a/solution.py
+++ b/solution.py
@@ -3,7 +3,6 @@
 
 import jax
 import jax.numpy as jnp
-import numpy as np
 from jax import lax
 from jax.experimental import pallas as pl
 from jax.experimental.pallas import tpu as pltpu
@@ -16,25 +15,9 @@
 MESH = pl.DeviceIdType.MESH
 
 
-def table_factors(local_chans, rows):
-    sections = local_chans.bit_length() - 1
-    left = np.zeros((rows, sections, rows), np.float32)
-    right = np.zeros((sections, rows, local_chans), np.float32)
-    r = np.arange(rows)[:, None]
-    j = np.arange(rows)
-    c = np.arange(local_chans)[None, :]
-    for section in range(1, sections + 1):
-        trials = max(1, 2 ** (section - 2))
-        left[:, section - 1, :] = (j[None, :] % trials) == (r % trials)
-        band = c >> max(section, 2)
-        upper = (c >> (section - 1)) & 1
-        right[section - 1] = ((j[:, None] // trials) == band) & (upper == 1)
-    return left.reshape(rows, -1), right.reshape(-1, local_chans)
-
-
 def kernel(
-    sizes, fb_ref, total_ref, lag_ref, width_ref, out_ref, peak_ref,
-    held, rims, box_rim, spill, ext, weight, band, fb,
+    sizes, fb_ref, delay_ref, width_ref, out_ref, peak_ref,
+    held, rims, box_rim, spill, ext, weight, lags_of, band, fb,
     send_sem, recv_sem, rim_send, rim_recv, spill_send, spill_recv, in_sem, out_sem,
 ):
     beams, chans, length, rows, per, merges, times = sizes
@@ -73,10 +56,32 @@
 
     load(0).start()
 
+    sections = chans.bit_length() - 1
+    grid = lambda shape, axis: lax.broadcasted_iota(jnp.int32, shape, axis)
+    flag = lambda test: jnp.where(test, 1.0, 0.0)
+    total = jnp.zeros((rows, chans), jnp.float32)
+    for section in range(1, sections + 1):
+        trials = max(1, 2 ** (section - 2))
+        entry, trial = grid((rows, rows), 1), grid((rows, rows), 0)
+        same = flag((entry & (trials - 1)) == (trial & (trials - 1)))
+        picked = same * delay_ref[section - 1 : section, :].astype(jnp.float32)
+        entry, chan = grid((rows, chans), 0), grid((rows, chans), 1)
+        band_of = lax.shift_right_logical(entry, max(section, 2) - 2) == lax.shift_right_logical(chan, max(section, 2))
+        upper = (lax.shift_right_logical(chan, section - 1) & 1) == 1
+        total = total + jnp.dot(
+            picked.astype(jnp.bfloat16), flag(band_of & upper).astype(jnp.bfloat16), preferred_element_type=jnp.float32
+        )
     for q in range(split):
-        total = total_ref[q * per : (q + 1) * per, :]
-        for s in range(shifts):
-            weight[q, s] = (total == float(s)).astype(jnp.bfloat16)
+        part = total[q * per : (q + 1) * per, :]
+        for s in range(0, shifts, 2):
+            pair = jnp.concatenate([flag(part == float(s)), flag(part == float(s + 1))], axis=0)
+            weight[q, s * per : (s + 2) * per, :] = pair.astype(jnp.bfloat16)
+    own = flag(grid((rows, rows), 0) == grid((rows, rows), 1))
+    for m in range(merges):
+        picked = own * delay_ref[sections + m : sections + m + 1, :].astype(jnp.float32)
+        lags_of[m] = jnp.dot(
+            picked.astype(jnp.bfloat16), jnp.ones((rows, TILE), jnp.bfloat16), preferred_element_type=jnp.float32
+        )
     gap = lax.broadcasted_iota(jnp.int32, (2 * TILE, TILE), 0) - lax.broadcasted_iota(jnp.int32, (2 * TILE, TILE), 1)
     for w in range(widths):
         band[:, w * TILE : (w + 1) * TILE] = ((gap >= 0) & (gap < width_ref[w])).astype(jnp.float32).astype(jnp.bfloat16)
@@ -144,7 +149,7 @@
             spill_copy(c - 2).wait_send()
 
         ext[side] = jnp.zeros(ext.shape[1:], jnp.float32)
-        mat = weight[q].reshape(shifts * per, chans)
+        mat = weight[q]
         step = BLOCK // 2
 
         def columns(k, carry):
@@ -155,7 +160,7 @@
                 ext[side, :, to] = ext[side, :, to] + part[s * per : (s + 1) * per, :]
             return carry
 
-        lax.fori_loop(0, length // step, columns, 0)
+        lax.fori_loop(0, length // step, columns, 0, unroll=2)
 
         @pl.when(has_left)
         def _():
@@ -192,7 +197,7 @@
         low = is_upper[m] * (m + 1)
         high = (1 - is_upper[m]) * (m + 1)
         _, at = place(c)
-        lag = jnp.concatenate([lag_ref[m, at, :]] * (BLOCK // TILE), axis=1)
+        lag = jnp.concatenate([lags_of[m, at, :]] * (BLOCK // TILE), axis=1)
         last = m == merges - 1
         for start in range(0, length, BLOCK):
             if start + BLOCK < length:
@@ -201,7 +206,7 @@
                 window = jnp.concatenate([held[high, c, :, start : start + BLOCK], rims[m, c]], axis=1)
             moved = window[:, :BLOCK]
             for offset in range(1, DMAX + 1):
-                moved = jnp.where(lag == offset, window[:, offset * TILE : offset * TILE + BLOCK], moved)
+                moved = jnp.where(lag == float(offset), window[:, offset * TILE : offset * TILE + BLOCK], moved)
             new = held[low, c, :, start : start + BLOCK] + moved
             if last:
                 new = new * jnp.float32(1.0 / math.sqrt(CHANS))
@@ -223,20 +228,19 @@
         beam, at = place(c)
         lane = lax.broadcasted_iota(jnp.int32, (per, TILE), 1)
         found = [jnp.zeros((per, TILE), jnp.float32) for _ in range(widths)]
-        group = min(8, tiles)
+        group = min(16, tiles)
         for first in range(0, tiles, group):
             start = first * TILE
             if first + group < tiles:
                 window = held[0, c, :, start : start + (group + 1) * TILE]
             else:
                 window = jnp.concatenate([held[0, c, :, start : start + group * TILE], box_rim[c]], axis=1)
-            coarse = window.astype(jnp.bfloat16)
-            fine = (window - coarse.astype(jnp.float32)).astype(jnp.bfloat16)
-            pairs = [
-                jnp.concatenate([part[:, i * TILE : (i + 2) * TILE] for i in range(group)], axis=0)
-                for part in (coarse, fine)
-            ]
-            sums = sum(jnp.dot(pair, band[...], preferred_element_type=jnp.float32) for pair in pairs)
+            pairs = jnp.concatenate([window[:, i * TILE : (i + 2) * TILE] for i in range(group)], axis=0)
+            coarse = pairs.astype(jnp.bfloat16)
+            fine = (pairs - coarse.astype(jnp.float32)).astype(jnp.bfloat16)
+            both = jnp.concatenate([coarse, fine], axis=0)
+            sums = jnp.dot(both, band[...], preferred_element_type=jnp.float32)
+            sums = sums[: group * per] + sums[group * per :]
             for w in range(widths):
                 best = jnp.max(sums[:, w * TILE : (w + 1) * TILE], axis=1, keepdims=True)
                 for i in range(group):
@@ -246,7 +250,7 @@
             peak_ref[w, beam, at, :] = (found[w] * (1.0 / jnp.sqrt(span)))[:, :tiles]
 
     lags = [3 + 2 * m for m in range(merges)]
-    lags[-1] += 1
+    lags[-1] += 3
     final = lags[-1] + 1
 
     def step(i, carry):
@@ -284,32 +288,46 @@
     lax.fori_loop(0, chunks, drain, 0)
 
 
+def hand_over(series_ref, peak_ref, series_out, peak_out, sems):
+    widths, beams = peak_ref.shape[:2]
+    copies = [pltpu.make_async_copy(series_ref.at[b], series_out.at[b], sems.at[b]) for b in range(beams)]
+    for copy in copies:
+        copy.start()
+
+    def turn(b, carry):
+        for w in range(widths):
+            peak_out[w, b] = peak_ref[w, b].T
+        return carry
+
+    lax.fori_loop(0, beams, turn, 0)
+    for copy in copies:
+        copy.wait()
+
+
 def shards(filterbank, delays, widths):
     beams, chans, length = filterbank.shape
     rows = chans // 4
-    per = min(rows, 16)
+    per = 8
     chunks = beams * (rows // per)
     local_sections = chans.bit_length() - 1
     merges = lax.axis_size("chan").bit_length() - 1
     times = lax.axis_size("tm")
     tiles = length // TILE
     depth = DMAX * local_sections
-    left, right = table_factors(chans, rows)
-    table = delays[:local_sections].reshape(-1, 1).astype(jnp.bfloat16) * jnp.asarray(right, jnp.bfloat16)
-    total = jnp.dot(jnp.asarray(left, jnp.bfloat16), table, preferred_element_type=jnp.float32)
-    lag = jnp.broadcast_to(delays[local_sections:, :, None], (merges, rows, TILE))
+    stacked = (depth // 2 + 1) * 2 * per
     sizes = (beams, chans, length, rows, per, merges, times)
     f32 = jnp.float32
     vmem = pl.BlockSpec(memory_space=pltpu.VMEM)
     hbm = pl.BlockSpec(memory_space=pl.ANY)
     dma = pltpu.SemaphoreType.DMA
-    return pl.pallas_call(
+    shapes = (
+        jax.ShapeDtypeStruct((beams, rows, length), f32),
+        jax.ShapeDtypeStruct((widths.shape[0], beams, rows, tiles), f32),
+    )
+    results = pl.pallas_call(
         functools.partial(kernel, sizes),
-        out_shape=(
-            jax.ShapeDtypeStruct((beams, rows, length), f32),
-            jax.ShapeDtypeStruct((widths.shape[0], beams, rows, tiles), f32),
-        ),
-        in_specs=[hbm, vmem, vmem, pl.BlockSpec(memory_space=pltpu.SMEM)],
+        out_shape=shapes,
+        in_specs=[hbm, vmem, pl.BlockSpec(memory_space=pltpu.SMEM)],
         out_specs=(hbm, vmem),
         scratch_shapes=[
             pltpu.VMEM((merges + 1, chunks, per, length), f32),
@@ -317,7 +335,8 @@
             pltpu.VMEM((chunks, per, TILE), f32),
             pltpu.VMEM((chunks, per, depth * TILE), f32),
             pltpu.VMEM((2, per, depth * TILE + length), f32),
-            pltpu.VMEM((rows // per, depth + 1, per, chans), jnp.bfloat16),
+            pltpu.VMEM((rows // per, stacked, chans), jnp.bfloat16),
+            pltpu.VMEM((merges, rows, TILE), f32),
             pltpu.VMEM((2 * TILE, widths.shape[0] * TILE), jnp.bfloat16),
             pltpu.VMEM((2, chans, length), jnp.bfloat16),
             dma((merges, chunks)),
@@ -333,7 +352,18 @@
             collective_id=0, has_side_effects=True, vmem_limit_bytes=60 * 2**20
         ),
         name="dedisperse",
-    )(filterbank, total, lag, widths)
+    )(filterbank, delays, widths)
+    turned = (widths.shape[0], beams, tiles, rows)
+    series, peaks = pl.pallas_call(
+        hand_over,
+        out_shape=(shapes[0], jax.ShapeDtypeStruct(turned, f32)),
+        in_specs=[hbm, vmem],
+        out_specs=(hbm, vmem),
+        scratch_shapes=[dma((beams,))],
+        compiler_params=pltpu.CompilerParams(vmem_limit_bytes=60 * 2**20),
+        name="hand_over",
+    )(*results)
+    return series, jnp.swapaxes(peaks, 2, 3)
 
 
 def solution(mesh):

time: 426 us -> 664 us (1.56)
  Pallas kernels: 410 us -> 663 us
  local copies, waits for them, and re-layouts: 12.5 us -> 0 us
    pallas_call x1 -> x2, Pallas kernels: 410 us -> 663 us  [the longest x1 406 us: shards(): pl.pallas_call(functools.partial(kernel, sizes), out_shape=shapes, in_spe...]
    unnamed x1 -> x0, local copies, waits for them, and re-layouts: 7.77 us -> none
where the time goes in v2:
time: 664 us
  Pallas kernels  663 us (100%)
    pallas_call x1, Pallas kernels, shards(): pl.pallas_call(functools.partial(kernel, sizes), out_shape=shapes, in_spe...  406 us
    pallas_call x1, Pallas kernels, shards(): pl.pallas_call(hand_over, out_shape=(shapes[0], jax.ShapeDtypeStruct(turn...  258 us

profile of v2, /device:TPU:0, one launch (start us, length us, event | category | flops | bytes accessed | tf_op | source)
XLA Modules:
  0.0 664.1 jit_solution(563944348547029035)
XLA Ops:
  0.6 405.6 %dedisperse.1 = (f32[8,64,4096]{2,1,0:T(8,128)}, f32[8,8,64,32]{3,2,1,0:T(8,128)}) custom-call(bf16[8,256,4096]{2,1,0:T(8,128)(2,1)} %fb_ref.1, s32[12,64]{1,0:T(8,128)} %delay_ref.1, s32[8]{0:T(128)} %width_ref.1), custom_call_target="tpu_custom_call" | custom-call | tf_op jit(solution)/shard_map/dedisperse/pallas_call | solution.py:327
  406.2 257.8 %hand_over.1 = (f32[8,64,4096]{2,1,0:T(8,128)}, f32[8,8,32,64]{3,2,1,0:T(8,128)}) custom-call(f32[8,64,4096]{2,1,0:T(8,128)} %get-tuple-element.6.series_ref, f32[8,8,64,32]{3,2,1,0:T(8,128)} %get-tuple-element.7.peak_ref), custom_call_target="tpu_custom_call" | custom-call | tf_op jit(solution)/shard_map/hand_over/pallas_call | solution.py:357

commit v3 on v2

--- a/solution.py
+++ b/solution.py
@@ -11,7 +11,7 @@
 CHANS = 4096
 TILE = 128
 DMAX = 2
-BLOCK = 1024
+BLOCK = 16
 MESH = pl.DeviceIdType.MESH
 
 
@@ -26,8 +26,6 @@
     tiles = length // TILE
     depth = DMAX * (chans.bit_length() - 1)
     shifts = depth + 1
-    lead = depth * TILE
-    rim = DMAX * TILE
     widths = width_ref.shape[0]
     me = lax.axis_index("chan")
     now = lax.axis_index("tm")
@@ -73,9 +71,10 @@
         )
     for q in range(split):
         part = total[q * per : (q + 1) * per, :]
-        for s in range(0, shifts, 2):
-            pair = jnp.concatenate([flag(part == float(s)), flag(part == float(s + 1))], axis=0)
-            weight[q, s * per : (s + 2) * per, :] = pair.astype(jnp.bfloat16)
+        for p in range(0, shifts, 2):
+            s = depth - p
+            pair = jnp.concatenate([flag(part == float(s)), flag(part == float(s - 1))], axis=0)
+            weight[q, p * per : (p + 2) * per, :] = pair.astype(jnp.bfloat16)
     own = flag(grid((rows, rows), 0) == grid((rows, rows), 1))
     for m in range(merges):
         picked = own * delay_ref[sections + m : sections + m + 1, :].astype(jnp.float32)
@@ -104,21 +103,21 @@
     def rim_copy(m, c):
         slot = (1 - is_upper[m]) * (m + 1)
         return pltpu.make_async_remote_copy(
-            src_ref=held.at[slot, c, :, pl.ds(0, rim)], dst_ref=rims.at[m, c],
+            src_ref=held.at[slot, c, pl.ds(0, DMAX)], dst_ref=rims.at[m, c],
             send_sem=rim_send.at[m, c], recv_sem=rim_recv.at[m, c],
             device_id={"tm": left}, device_id_type=MESH,
         )
 
     def box_copy(c):
         return pltpu.make_async_remote_copy(
-            src_ref=held.at[0, c, :, pl.ds(0, TILE)], dst_ref=box_rim.at[c],
+            src_ref=held.at[0, c, pl.ds(0, 1)], dst_ref=box_rim.at[c],
             send_sem=rim_send.at[merges, c], recv_sem=rim_recv.at[merges, c],
             device_id={"tm": left}, device_id_type=MESH,
         )
 
     def spill_copy(c):
         return pltpu.make_async_remote_copy(
-            src_ref=ext.at[lax.rem(c, 2), :, pl.ds(0, lead)], dst_ref=spill.at[c],
+            src_ref=ext.at[lax.rem(c, 2), pl.ds(0, depth)], dst_ref=spill.at[c],
             send_sem=spill_send.at[c], recv_sem=spill_recv.at[c],
             device_id={"tm": left}, device_id_type=MESH,
         )
@@ -127,8 +126,7 @@
         return c // split, pl.ds(pl.multiple_of(lax.rem(c, split) * per, per), per)
 
     def result(c):
-        beam, at = place(c)
-        return pltpu.make_async_copy(held.at[0, c], out_ref.at[beam, at, :], out_sem.at[c])
+        return pltpu.make_async_copy(held.at[0, c], out_ref.at[c // split, lax.rem(c, split)], out_sem.at[c])
 
     def local(c):
         beam = c // split
@@ -150,29 +148,37 @@
 
         ext[side] = jnp.zeros(ext.shape[1:], jnp.float32)
         mat = weight[q]
-        step = BLOCK // 2
+        group = 4
 
         def columns(k, carry):
-            at = pl.multiple_of(k * step, step)
-            part = jnp.dot(mat, fb[slot, :, pl.ds(at, step)], preferred_element_type=jnp.float32)
-            for s in range(shifts):
-                to = pl.ds(pl.multiple_of(at + (depth - s) * TILE, TILE), step)
-                ext[side, :, to] = ext[side, :, to] + part[s * per : (s + 1) * per, :]
+            at = pl.multiple_of(k * (group * TILE), group * TILE)
+            part = jnp.dot(mat, fb[slot, :, pl.ds(at, group * TILE)], preferred_element_type=jnp.float32)
+            sums = []
+            for j in range(group):
+                block = part[: shifts * per, j * TILE : (j + 1) * TILE].reshape(shifts, per, TILE)
+                ends = [jnp.zeros((n, per, TILE), jnp.float32) for n in (j, group - 1 - j) if n > 0]
+                if j > 0:
+                    block = jnp.concatenate([ends[0], block], axis=0)
+                if j < group - 1:
+                    block = jnp.concatenate([block, ends[-1]], axis=0)
+                sums.append(block)
+            to = pl.ds(k * group, depth + group)
+            ext[side, to] = ext[side, to] + ((sums[0] + sums[1]) + (sums[2] + sums[3]))
             return carry
 
-        lax.fori_loop(0, length // step, columns, 0, unroll=2)
+        lax.fori_loop(0, tiles // group, columns, 0, unroll=2)
 
         @pl.when(has_left)
         def _():
             spill_copy(c).start()
 
-        held[0, c] = ext[side, :, lead:]
+        held[0, c] = ext[side, depth:]
 
     def join(c):
         @pl.when(has_right)
         def _():
             spill_copy(c).wait_recv()
-            held[0, c, :, length - lead :] = held[0, c, :, length - lead :] + spill[c]
+            held[0, c, tiles - depth :] = held[0, c, tiles - depth :] + spill[c]
 
         exchange(0, c).start()
 
@@ -197,20 +203,21 @@
         low = is_upper[m] * (m + 1)
         high = (1 - is_upper[m]) * (m + 1)
         _, at = place(c)
-        lag = jnp.concatenate([lags_of[m, at, :]] * (BLOCK // TILE), axis=1)
+        lag = lags_of[m, at, :][None]
         last = m == merges - 1
-        for start in range(0, length, BLOCK):
-            if start + BLOCK < length:
-                window = held[high, c, :, start : start + BLOCK + rim]
+        for start in range(0, tiles, BLOCK):
+            end = start + BLOCK
+            if end < tiles:
+                window = held[high, c, start : end + DMAX]
             else:
-                window = jnp.concatenate([held[high, c, :, start : start + BLOCK], rims[m, c]], axis=1)
-            moved = window[:, :BLOCK]
+                window = jnp.concatenate([held[high, c, start:end], rims[m, c]], axis=0)
+            moved = window[:BLOCK]
             for offset in range(1, DMAX + 1):
-                moved = jnp.where(lag == float(offset), window[:, offset * TILE : offset * TILE + BLOCK], moved)
-            new = held[low, c, :, start : start + BLOCK] + moved
+                moved = jnp.where(lag == float(offset), window[offset : offset + BLOCK], moved)
+            new = held[low, c, start:end] + moved
             if last:
                 new = new * jnp.float32(1.0 / math.sqrt(CHANS))
-            held[0, c, :, start : start + BLOCK] = new
+            held[0, c, start:end] = new
         if last:
             result(c).start()
 
@@ -230,12 +237,11 @@
         found = [jnp.zeros((per, TILE), jnp.float32) for _ in range(widths)]
         group = min(16, tiles)
         for first in range(0, tiles, group):
-            start = first * TILE
             if first + group < tiles:
-                window = held[0, c, :, start : start + (group + 1) * TILE]
+                window = held[0, c, first : first + group + 1]
             else:
-                window = jnp.concatenate([held[0, c, :, start : start + group * TILE], box_rim[c]], axis=1)
-            pairs = jnp.concatenate([window[:, i * TILE : (i + 2) * TILE] for i in range(group)], axis=0)
+                window = jnp.concatenate([held[0, c, first : first + group], box_rim[c]], axis=0)
+            pairs = jnp.concatenate([window[:group], window[1:]], axis=2).reshape(group * per, 2 * TILE)
             coarse = pairs.astype(jnp.bfloat16)
             fine = (pairs - coarse.astype(jnp.float32)).astype(jnp.bfloat16)
             both = jnp.concatenate([coarse, fine], axis=0)
@@ -288,20 +294,13 @@
     lax.fori_loop(0, chunks, drain, 0)
 
 
-def hand_over(series_ref, peak_ref, series_out, peak_out, sems):
-    widths, beams = peak_ref.shape[:2]
-    copies = [pltpu.make_async_copy(series_ref.at[b], series_out.at[b], sems.at[b]) for b in range(beams)]
-    for copy in copies:
-        copy.start()
-
-    def turn(b, carry):
-        for w in range(widths):
-            peak_out[w, b] = peak_ref[w, b].T
-        return carry
-
-    lax.fori_loop(0, beams, turn, 0)
-    for copy in copies:
-        copy.wait()
+def hand_over(series_ref, peak_ref, series_out, peak_out):
+    _, split, tiles, per, _ = series_ref.shape
+    for i in range(tiles):
+        for q in range(split):
+            series_out[0, q * per : (q + 1) * per, i * TILE : (i + 1) * TILE] = series_ref[0, q, i]
+    for w in range(peak_ref.shape[0]):
+        peak_out[w, 0] = peak_ref[w, 0].T
 
 
 def shards(filterbank, delays, widths):
@@ -320,9 +319,11 @@
     vmem = pl.BlockSpec(memory_space=pltpu.VMEM)
     hbm = pl.BlockSpec(memory_space=pl.ANY)
     dma = pltpu.SemaphoreType.DMA
+    split = rows // per
+    spans = widths.shape[0]
     shapes = (
-        jax.ShapeDtypeStruct((beams, rows, length), f32),
-        jax.ShapeDtypeStruct((widths.shape[0], beams, rows, tiles), f32),
+        jax.ShapeDtypeStruct((beams, split, tiles, per, TILE), f32),
+        jax.ShapeDtypeStruct((spans, beams, rows, tiles), f32),
     )
     results = pl.pallas_call(
         functools.partial(kernel, sizes),
@@ -330,11 +331,11 @@
         in_specs=[hbm, vmem, pl.BlockSpec(memory_space=pltpu.SMEM)],
         out_specs=(hbm, vmem),
         scratch_shapes=[
-            pltpu.VMEM((merges + 1, chunks, per, length), f32),
-            pltpu.VMEM((merges, chunks, per, DMAX * TILE), f32),
-            pltpu.VMEM((chunks, per, TILE), f32),
-            pltpu.VMEM((chunks, per, depth * TILE), f32),
-            pltpu.VMEM((2, per, depth * TILE + length), f32),
+            pltpu.VMEM((merges + 1, chunks, tiles, per, TILE), f32),
+            pltpu.VMEM((merges, chunks, DMAX, per, TILE), f32),
+            pltpu.VMEM((chunks, 1, per, TILE), f32),
+            pltpu.VMEM((chunks, depth, per, TILE), f32),
+            pltpu.VMEM((2, depth + tiles, per, TILE), f32),
             pltpu.VMEM((rows // per, stacked, chans), jnp.bfloat16),
             pltpu.VMEM((merges, rows, TILE), f32),
             pltpu.VMEM((2 * TILE, widths.shape[0] * TILE), jnp.bfloat16),
@@ -353,13 +354,21 @@
         ),
         name="dedisperse",
     )(filterbank, delays, widths)
-    turned = (widths.shape[0], beams, tiles, rows)
     series, peaks = pl.pallas_call(
         hand_over,
-        out_shape=(shapes[0], jax.ShapeDtypeStruct(turned, f32)),
-        in_specs=[hbm, vmem],
-        out_specs=(hbm, vmem),
-        scratch_shapes=[dma((beams,))],
+        grid=(beams,),
+        out_shape=(
+            jax.ShapeDtypeStruct((beams, rows, length), f32),
+            jax.ShapeDtypeStruct((spans, beams, tiles, rows), f32),
+        ),
+        in_specs=[
+            pl.BlockSpec((1, split, tiles, per, TILE), lambda b: (b, 0, 0, 0, 0)),
+            pl.BlockSpec((spans, 1, rows, tiles), lambda b: (0, b, 0, 0)),
+        ],
+        out_specs=(
+            pl.BlockSpec((1, rows, length), lambda b: (b, 0, 0)),
+            pl.BlockSpec((spans, 1, tiles, rows), lambda b: (0, b, 0, 0)),
+        ),
         compiler_params=pltpu.CompilerParams(vmem_limit_bytes=60 * 2**20),
         name="hand_over",
     )(*results)

time: 664 us -> 413 us (0.62)
  Pallas kernels: 663 us -> 412 us
    pallas_call x1, Pallas kernels: 258 us -> 9.66 us  [shards(): pl.pallas_call(hand_over, grid=(beams,), out_shape=(jax.ShapeDtypeStruct(...]
where the time goes in v3:
time: 413 us
  Pallas kernels  412 us (100%)
    pallas_call x1, Pallas kernels, shards(): pl.pallas_call(functools.partial(kernel, sizes), out_shape=shapes, in_spe...  402 us
    pallas_call x1, Pallas kernels, shards(): pl.pallas_call(hand_over, grid=(beams,), out_shape=(jax.ShapeDtypeStruct(...  9.66 us

profile of v3, /device:TPU:0, one launch (start us, length us, event | category | flops | bytes accessed | tf_op | source)
XLA Modules:
  0.0 412.5 jit_solution(2505379027439245218)
XLA Ops:
  0.6 402.2 %dedisperse.1 = (f32[8,8,32,8,128]{4,3,2,1,0:T(8,128)}, f32[8,8,64,32]{3,2,1,0:T(8,128)}) custom-call(bf16[8,256,4096]{2,1,0:T(8,128)(2,1)} %fb_ref.1, s32[12,64]{1,0:T(8,128)} %delay_ref.1, s32[8]{0:T(128)} %width_ref.1), custom_call_target="tpu_custom_call" | custom-call | tf_op jit(solution)/shard_map/dedisperse/pallas_call | solution.py:328
  402.8 9.7 %hand_over.1 = (f32[8,64,4096]{2,1,0:T(8,128)}, f32[8,8,32,64]{3,2,1,0:T(8,128)}) custom-call(f32[8,8,32,8,128]{4,3,2,1,0:T(8,128)} %get-tuple-element.6.series_ref, f32[8,8,64,32]{3,2,1,0:T(8,128)} %get-tuple-element.7.peak_ref), custom_call_target="tpu_custom_call" | custom-call | tf_op jit(solution)/shard_map/hand_over/pallas_call | solution.py:357

commit v4 on v3

--- a/solution.py
+++ b/solution.py
@@ -295,12 +295,14 @@
 
 
 def hand_over(series_ref, peak_ref, series_out, peak_out):
-    _, split, tiles, per, _ = series_ref.shape
-    for i in range(tiles):
+    held, split, tiles, per, _ = series_ref.shape
+    spans, _, rows, _ = peak_ref.shape
+    turned = jnp.swapaxes(peak_ref[...].reshape(spans * held, rows, tiles), 1, 2)
+    peak_out[...] = turned.reshape(spans, held, tiles, rows)
+    for b in range(held):
         for q in range(split):
-            series_out[0, q * per : (q + 1) * per, i * TILE : (i + 1) * TILE] = series_ref[0, q, i]
-    for w in range(peak_ref.shape[0]):
-        peak_out[w, 0] = peak_ref[w, 0].T
+            for i in range(tiles):
+                series_out[b, q * per : (q + 1) * per, i * TILE : (i + 1) * TILE] = series_ref[b, q, i]
 
 
 def shards(filterbank, delays, widths):
@@ -356,18 +358,18 @@
     )(filterbank, delays, widths)
     series, peaks = pl.pallas_call(
         hand_over,
-        grid=(beams,),
+        grid=(beams // 2,),
         out_shape=(
             jax.ShapeDtypeStruct((beams, rows, length), f32),
             jax.ShapeDtypeStruct((spans, beams, tiles, rows), f32),
         ),
         in_specs=[
-            pl.BlockSpec((1, split, tiles, per, TILE), lambda b: (b, 0, 0, 0, 0)),
-            pl.BlockSpec((spans, 1, rows, tiles), lambda b: (0, b, 0, 0)),
+            pl.BlockSpec((2, split, tiles, per, TILE), lambda b: (b, 0, 0, 0, 0)),
+            pl.BlockSpec((spans, 2, rows, tiles), lambda b: (0, b, 0, 0)),
         ],
         out_specs=(
-            pl.BlockSpec((1, rows, length), lambda b: (b, 0, 0)),
-            pl.BlockSpec((spans, 1, tiles, rows), lambda b: (0, b, 0, 0)),
+            pl.BlockSpec((2, rows, length), lambda b: (b, 0, 0)),
+            pl.BlockSpec((spans, 2, tiles, rows), lambda b: (0, b, 0, 0)),
         ),
         compiler_params=pltpu.CompilerParams(vmem_limit_bytes=60 * 2**20),
         name="hand_over",

time: 413 us -> 411 us (level)
  no operation moved by 1% of the time
where the time goes in v4:
time: 411 us
  Pallas kernels  410 us (100%)
    pallas_call x1, Pallas kernels, shards(): pl.pallas_call(functools.partial(kernel, sizes), out_shape=shapes, in_spe...  402 us

profile of v4, /device:TPU:0, one launch (start us, length us, event | category | flops | bytes accessed | tf_op | source)
XLA Modules:
  0.0 410.7 jit_solution(479205449926163399)
XLA Ops:
  0.6 402.2 %dedisperse.1 = (f32[8,8,32,8,128]{4,3,2,1,0:T(8,128)}, f32[8,8,64,32]{3,2,1,0:T(8,128)}) custom-call(bf16[8,256,4096]{2,1,0:T(8,128)(2,1)} %fb_ref.1, s32[12,64]{1,0:T(8,128)} %delay_ref.1, s32[8]{0:T(128)} %width_ref.1), custom_call_target="tpu_custom_call" | custom-call | tf_op jit(solution)/shard_map/dedisperse/pallas_call | solution.py:330
  402.8 7.9 %hand_over.1 = (f32[8,64,4096]{2,1,0:T(8,128)}, f32[8,8,32,64]{3,2,1,0:T(8,128)}) custom-call(f32[8,8,32,8,128]{4,3,2,1,0:T(8,128)} %get-tuple-element.6.series_ref, f32[8,8,64,32]{3,2,1,0:T(8,128)} %get-tuple-element.7.peak_ref), custom_call_target="tpu_custom_call" | custom-call | tf_op jit(solution)/shard_map/hand_over/pallas_call | solution.py:359
